TPU v7x, 256 devices: a whole 4x4x8 slice. The times are simulated.
256 devices in a mesh: seq: 32 (over x_lo, z, core), kvh: 8 (over x_hi, y).
Axes of the slice: x: 4 (x_hi: 2, x_lo: 2; x = x_hi * 2 + x_lo), y: 4, z: 8, core: 2. Of those that a mesh axis runs over, the one named last changes fastest.
Arguments:
- queries: bfloat16 [32768, 4096], P('seq', 'kvh'), may hold values from -8 to 8
- keys: bfloat16 [32768, 1024], P('seq', 'kvh'), may hold values from -8 to 8
- values: bfloat16 [32768, 1024], P('seq', 'kvh'), may hold values from -6 to 6
- out_weight: bfloat16 [4096, 4096], P('kvh'), may hold values from -0.09375 to 0.09375
Outputs:
- mixed: bfloat16 [32768, 4096], P('seq', 'kvh')
- log_total: float32 [32, 32768], P('kvh', 'seq')
All inputs are finite; a program needn't handle non-finite values.
Results may differ from a plain program's by a relative error of at most 0.015.
Values may be sent and summed in bfloat16 or wider, within the bound.
A program may use at most 64 MiB of HBM per device.

v0:
```python
import jax
import jax.numpy as jnp
from jax import lax
from jax.sharding import PartitionSpec as P

HEADS = 32
KV_HEADS = 8
HEAD_DIM = 128


def passed_along(value, axis, steps):
    count = lax.axis_size(axis)
    initial, last = (max(0, -steps), min(count, count - steps))
    return lax.ppermute(value, axis, [(source, source + steps) for source in range(initial, last)])


def tile(query, key_rows, value_rows, mask):
    scale = HEAD_DIM ** (-0.5)
    scores = (
        jnp.einsum("tkgd,skd->kgts", query, key_rows, preferred_element_type=jnp.float32) * scale
    )
    scores = jnp.where(mask, scores, -1e30)
    top = jnp.max(scores, axis=-1)
    weights = jnp.where(mask, jnp.exp(scores - top[..., None]), 0.0)
    total = jnp.sum(weights, axis=-1)
    acc = jnp.einsum(
        "kgts,skd->kgtd",
        weights.astype(jnp.bfloat16),
        value_rows,
        preferred_element_type=jnp.float32,
    )
    return (acc, top, total)


def combine(results):
    top = results[0][1]
    for item in results[1:]:
        top = jnp.maximum(top, item[1])
    total = jnp.zeros_like(top)
    acc = jnp.zeros_like(results[0][0])
    for item in results:
        factor = jnp.exp(item[1] - top)
        total = total + factor * item[2]
        acc = acc + factor[..., None] * item[0]
    return (acc, top, total)


def body(queries, keys, values, out_weight):
    tokens = queries.shape[0]
    half = tokens // 2
    group = HEADS // KV_HEADS
    kv_local = keys.shape[1] // HEAD_DIM
    query = queries.reshape(tokens, kv_local, group, HEAD_DIM)
    key_rows = keys.reshape(tokens, kv_local, HEAD_DIM)
    value_rows = values.reshape(tokens, kv_local, HEAD_DIM)
    blocks = lax.axis_size("seq")
    offset = blocks // 2
    index = lax.axis_index("seq")
    busy = index >= offset
    qpos = jnp.arange(tokens, dtype=jnp.int32)
    full = jnp.ones((tokens, half), bool)
    results = []
    for part in range(2):
        kpos = jnp.arange(half, dtype=jnp.int32) + part * half
        mask = qpos[:, None] >= kpos[None, :]
        results.append(
            tile(
                query,
                key_rows[part * half : (part + 1) * half],
                value_rows[part * half : (part + 1) * half],
                mask,
            )
        )
    empty = (
        jnp.zeros((kv_local, group, tokens, HEAD_DIM), jnp.float32),
        jnp.full((kv_local, group, tokens), -1e30, jnp.float32),
        jnp.zeros((kv_local, group, tokens), jnp.float32),
    )
    prev_keys, prev_values = passed_along((keys, values), "seq", offset)
    prev_k = prev_keys.reshape(tokens, kv_local, HEAD_DIM)
    prev_v = prev_values.reshape(tokens, kv_local, HEAD_DIM)

    def earlier():
        first = tile(query, prev_k[:half], prev_v[:half], full)
        second = tile(query, prev_k[half:], prev_v[half:], full)
        return combine([first, second])

    def nothing():
        return empty

    results.append(lax.cond(busy, earlier, nothing))
    acc, top, total = combine(results)
    attended = (
        (acc / total[..., None]).transpose(2, 0, 1, 3).reshape(tokens, kv_local * group * HEAD_DIM)
    )
    attended = attended.astype(jnp.bfloat16)
    log_total = (top + jnp.log(total)).reshape(kv_local * group, tokens)
    term = jnp.dot(attended, out_weight, preferred_element_type=jnp.float32)
    mixed = lax.psum_scatter(term.astype(jnp.bfloat16), "kvh", scatter_dimension=1, tiled=True)
    return (mixed, log_total)


def solution(mesh):
    in_specs = (P("seq", "kvh"), P("seq", "kvh"), P("seq", "kvh"), P("kvh", None))
    out_specs = (P("seq", "kvh"), P("kvh", "seq"))
    return jax.shard_map(body, mesh=mesh, in_specs=in_specs, out_specs=out_specs, check_vma=False)
```

profile of v0, /device:TPU:2, one launch (start us, length us, event | category | flops | bytes accessed | tf_op | source)
XLA Modules:
  0.0 179.8 jit_solution(10465277908438310269)
XLA Ops:
  7.2 0.0 copy-start.1
  7.2 0.0 reduce-scatter.2.cloned.1.call-start
  7.2 1.4 collective-permute-start
  8.7 1.3 collective-permute-start.1
  10.0 0.1 iota_compare_fusion.1
  10.1 0.4 iota_compare_fusion
  10.5 0.0 copy-start.2
  10.5 3.0 %fusion.39 = (f32[4,1024]{1,0:T(4,128)S(1)}, f32[512,1024,4]{1,0,2:T(8,128)S(1)}) fusion(pred[1024,512]{0,1:T(8,128)(4,1)S(1)} %iota_compare_fusion.1, bf16[1024,128]{1,0:T(8,128)(2,1)} %param.7, bf16[1024,512]{1,0:T(8,128)(2,1)} %param.6), kind=kOutput, calls=%fused_computation.52 | convolution fusion | flops 543158272 | bytes 10108928 | tf_op jit(solution)/shard_map/tkgd,skd->kgts/dot_general | solution.py:20
  13.5 1.6 fusion.40
  15.1 3.8 %fusion.47 = f32[4,1024,128]{1,2,0:T(8,128)} fusion(f32[512,1024,4]{1,0,2:T(8,128)S(1)} %get-tuple-element.40, f32[4,1024]{1,0:T(4,128)S(1)} %get-tuple-element.39, pred[1024,512]{0,1:T(8,128)(4,1)S(1)} %iota_compare_fusion.1, bf16[1024,128]{1,0:T(8,128)(2,1)S(1)} %copy-done.2), kind=kOutput, calls=%fused_computation.60 | convolution fusion | flops 547356672 | bytes 11157504 | tf_op jit(solution)/shard_map/kgts,skd->kgtd/dot_general | solution.py:26
  18.9 4.2 %fusion.41 = (f32[4,1024]{1,0:T(4,128)S(1)}, f32[4,1024]{1,0:T(4,128)S(1)}) fusion(f32[512,1024,4]{1,0,2:T(8,128)S(1)} %get-tuple-element.40, f32[4,1024]{1,0:T(4,128)S(1)} %get-tuple-element.39, pred[1024,512]{0,1:T(8,128)(4,1)S(1)} %iota_compare_fusion.1, f32[4,1024]{1,0:T(4,128)S(1)} %get-tuple-element.37, f32[512,1024,4]{1,0,2:T(8,128)S(1)} %get-tuple-element.38, ...), kind=kLoop, calls=%fused_computation.54 | loop fusion | flops 20963328 | bytes 17891328 | tf_op jit(solution)/shard_map/reduce_sum | solution.py:25
  23.1 3.8 %fusion.49 = f32[4,1024,128]{1,2,0:T(8,128)} fusion(f32[512,1024,4]{1,0,2:T(8,128)S(1)} %get-tuple-element.38, f32[4,1024]{1,0:T(4,128)S(1)} %get-tuple-element.37, pred[1024,512]{0,1:T(8,128)(4,1)S(1)} %iota_compare_fusion, bf16[1024,128]{1,0:T(8,128)(2,1)S(1)} %copy-done.2), kind=kOutput, calls=%fused_computation.61 | convolution fusion | flops 547356672 | bytes 11157504 | tf_op jit(solution)/shard_map/kgts,skd->kgtd/dot_general | solution.py:26
  26.9 11.3 %conditional.1 = (f32[1,4,1024]{2,1,0:T(4,128)S(1)}, f32[1,4,1024]{2,1,0:T(4,128)S(1)}, f32[1,4,1024,128]{2,3,1,0:T(8,128)}) conditional(s32[]{:T(128)} %convert_element_type.27, () %tuple.16, (bf16[1024,128]{1,0:T(8,128)(2,1)S(1)}, bf16[1024,512]{1,0:T(8,128)(2,1)S(1)}, bf16[1024,128]{1,0:T(8,128)(2,1)S(1)}) %tuple.37), branch_computations={%region_2.3_spmd, %region_3.8_spmd} | conditional | flops 2182631424 | bytes 63766552 | solution.py:91
  26.9 1.3 bitcast_reduce_fusion
  28.2 1.5 fusion.7
  29.8 1.3 bitcast_reduce_fusion.1
  31.0 2.8 %fusion.2 = (f32[4,1024]{1,0:T(4,128)S(1)}, f32[4,1024]{1,0:T(4,128)S(1)}) fusion(f32[512,1024,4]{1,0,2:T(8,128)S(1)} %get-tuple-element.31, f32[4,1024]{1,0:T(4,128)S(1)} %get-tuple-element.30, f32[4,1024]{1,0:T(4,128)S(1)} %get-tuple-element.28, f32[512,1024,4]{1,0,2:T(8,128)S(1)} %get-tuple-element.29), kind=kLoop, calls=%fused_computation.6 | loop fusion | flops 12574720 | bytes 16842752 | tf_op jit(solution)/shard_map/cond/branch_1_fun/reduce_sum | solution.py:25
  33.9 2.5 %add_bitcast_fusion = f32[1,4,1024,128]{3,2,1,0:T(8,128)S(1)} fusion(f32[4,1024,128]{2,1,0:T(8,128)S(1)} %fusion.7, f32[512,1024,4]{1,0,2:T(8,128)S(1)} %get-tuple-element.31, f32[4,1024]{1,0:T(4,128)S(1)} %get-tuple-element.30, f32[4,1024]{1,0:T(4,128)S(1)} %get-tuple-element.27, f32[4,1024]{1,0:T(4,128)S(1)} %get-tuple-element.26, ...), kind=kOutput, calls=%fused_computation.18 | convolution fusion | flops 544735232 | bytes 12763136 | tf_op jit(solution)/shard_map/cond/branch_1_fun/kgts,skd->kgtd/dot_general | solution.py:26
  36.4 1.9 %copy.22 = f32[1,4,1024,128]{2,3,1,0:T(8,128)} copy(f32[1,4,1024,128]{3,2,1,0:T(8,128)S(1)} %add_bitcast_fusion) | data formatting | bytes 4194304 | tf_op jit(solution)/shard_map/cond | solution.py:91
  38.3 0.6 add_bitcast_fusion.1
  39.0 3.7 %fusion.54 = bf16[1,4,1024,128]{2,3,1,0:T(8,128)(2,1)S(1)} fusion(f32[1,4,1024,128]{2,3,1,0:T(8,128)} %get-tuple-element.20, f32[4,1024,128]{1,2,0:T(8,128)} %fusion.49, f32[4,1024,128]{1,2,0:T(8,128)} %fusion.47, f32[4,1024]{1,0:T(4,128)S(1)} %bitcast.223, f32[4,1024]{1,0:T(4,128)S(1)} %get-tuple-element.35, f32[4,1024]{1,0:T(4,128)S(1)} %get-tuple-element.36, ...), kind=kLoop, calls=%fused_computation.66 | loop fusion | flops 3670016 | bytes 7405568 | tf_op jit(solution)/shard_map/convert_element_type | solution.py:96
  42.6 9.0 %convolution_convert_fusion = bf16[1024,4096]{1,0:T(8,128)(2,1)} fusion(bf16[1024,512]{0,1:T(8,128)(2,1)S(1)} %bitcast.222, bf16[512,4096]{1,0:T(8,128)(2,1)} %param.9), kind=kOutput, calls=%fused_computation.51 | convolution fusion | flops 4299161600 | bytes 13631488 | tf_op jit(solution)/shard_map/dot_general | solution.py:98
  51.6 0.0 reduce-scatter.2.cloned.1.call-update
  51.6 121.3 %reduce-scatter.2.cloned.1.call-done = bf16[1024,512]{1,0:T(8,128)(2,1)} async-done(((bf16[1024,4096]{1,0:T(8,128)(2,1)}), bf16[1024,512]{1,0:T(8,128)(2,1)}) %reduce-scatter.2.cloned.1.call-update) | async-done | bytes 1048592 | tf_op jit(solution)/shard_map/reduce_scatter | solution.py:99
  (10 shorter events, 0.1 us)
Async XLA Ops:
  7.2 6.3 %copy-start.1 = (bf16[1024,128]{1,0:T(8,128)(2,1)S(1)}, bf16[1024,128]{1,0:T(8,128)(2,1)}, u32[]{:S(2)}) copy-start(bf16[1024,128]{1,0:T(8,128)(2,1)} %param.7) | copy-start | bytes 786436
  7.2 6.3 %copy-start = (bf16[1024,512]{1,0:T(8,128)(2,1)S(1)}, bf16[1024,512]{1,0:T(8,128)(2,1)}, u32[]{:S(2)}) copy-start(bf16[1024,512]{1,0:T(8,128)(2,1)} %param.6) | copy-start | bytes 3145732
  7.2 165.8 %reduce-scatter.2.cloned.1.call-start = ((), (), s32[]{:S(2)}) async-start(), calls=%async_computation.1 | async-start | bytes 9437184 | tf_op jit(solution)/shard_map/reduce_scatter | solution.py:99
  7.2 19.7 %collective-permute-start = (bf16[1024,128]{1,0:T(8,128)(2,1)}, bf16[1024,128]{1,0:T(8,128)(2,1)S(1)}, u32[]{:S(2)}, u32[]{:S(2)}) collective-permute-start(bf16[1024,128]{1,0:T(8,128)(2,1)} %param.7), channel_id=1, source_target_pairs={{0,128},{8,136},{16,144},{24,152},{32,160},{40,168},{48,176},{56,1... | collective-permute-start | bytes 786440 | tf_op jit(solution)/shard_map/ppermute | solution.py:14
  8.7 18.3 %collective-permute-start.1 = (bf16[1024,128]{1,0:T(8,128)(2,1)}, bf16[1024,128]{1,0:T(8,128)(2,1)S(1)}, u32[]{:S(2)}, u32[]{:S(2)}) collective-permute-start(bf16[1024,128]{1,0:T(8,128)(2,1)} %param.8), channel_id=1, source_target_pairs={{0,128},{8,136},{16,144},{24,152},{32,160},{40,168},{48,176},{56,1... | collective-permute-start | bytes 786440 | tf_op jit(solution)/shard_map/ppermute | solution.py:14
  10.5 4.6 %copy-start.2 = (bf16[1024,128]{1,0:T(8,128)(2,1)S(1)}, bf16[1024,128]{1,0:T(8,128)(2,1)}, u32[]{:S(2)}) copy-start(bf16[1024,128]{1,0:T(8,128)(2,1)} %param.8) | copy-start | bytes 786436
Sparse Core Ops, SparseCore 0:
  51.7 121.1 reduce-scatter.1
where the time goes:
time: 181 us; the launch traced here: 180 us
  waiting for transfers between devices  121 us (67%)
  matrix products  27.7 us (15%)
  between operations  14.1 us (8%)
  other arithmetic  11.9 us (7%)
  starting transfers between devices  2.75 us (2%)
  local copies, waits for them, and re-layouts  1.88 us (1%)
    reduce_scatter x1, waiting for transfers between devices, body(): lax.psum_scatter(term.astype(jnp.bfloat16), 'kvh', scatter_dimension=1, t...  121 us
    dot_general x4, matrix products, tile(): jnp.einsum('kgts,skd->kgtd', weights.astype(jnp.bfloat16), value_rows, pr...  11.7 us
    dot_general x1, matrix products, body(): term = jnp.dot(attended, out_weight, preferred_element_type=jnp.float32)  8.96 us
    dot_general x4, matrix products, tile(): jnp.einsum('tkgd,skd->kgts', query, key_rows, preferred_element_type=jnp....  7.11 us
    reduce_sum x2, other arithmetic, tile(): total = jnp.sum(weights, axis=-1)  6.99 us
    convert_element_type x1, other arithmetic, body(): attended = attended.astype(jnp.bfloat16)  3.67 us
  transfers between devices with their start and end apart: 3, of which 1 were waited for; matrix products, arithmetic and copies ran while one was open for 9% of the time, Pallas kernels for 0%

commit v1 on v0

v1 whole, which is shorter than its diff:
```python
import functools
import math

import jax
import jax.numpy as jnp
from jax import lax
from jax.experimental import pallas as pl
from jax.experimental.pallas import tpu as pltpu
from jax.sharding import PartitionSpec as P

MESH = pl.DeviceIdType.MESH
HEAD = 128
GROUP = 4
TOK = 1024
QC = 256
FAR = 512
STEP = 128
NSTEP = TOK // STEP
BLK = 512
HALF = BLK // 2
WIDE = 4 * BLK
PIECE = 64
SCALE = math.log2(math.e) / math.sqrt(HEAD)
LN2 = math.log(2.0)
F32 = jnp.float32
BF16 = jnp.bfloat16


def dot_nt(a, b):
    return lax.dot_general(a, b, (((1,), (1,)), ((), ())), preferred_element_type=F32)


def dot_nn(a, b):
    return jnp.dot(a, b, preferred_element_type=F32)


def kernel(
    q_hbm, k_hbm, v_hbm, w_hbm, out_hbm, lse_hbm,
    q, k, v, kf, vf, wo, wr, att, attp, acc, top,
    m1s, m1r, m2s, m2r, outv, lsev,
    in_sem, out_sem, kv_ss, kv_rs, w_ss, w_rs, a_ss, a_rs, s1_ss, s1_rs, s2_ss, s2_rs,
):
    s = lax.axis_index("seq")
    g = lax.axis_index("kvh")
    xl, z, c = s // 16, (s // 2) % 8, s % 2
    xh, y = g // 4, g % 4
    busy = xl == 1

    def dev(xl=xl, z=z, c=c, xh=xh, y=y):
        return ((xl * 8 + z) * 2 + c, xh * 4 + y)

    d_kv = dev(xl=1 - xl)
    d_w = dev(xl=1 - xl, xh=1 - xh)
    d_z = [dev(z=(z + 1) % 8), dev(z=(z + 7) % 8), dev(z=(z + 2) % 8), dev(z=(z + 6) % 8)]
    d_c = dev(c=1 - c)
    d_a = dev(xh=1 - xh)
    d_y = [dev(y=(y + 1) % 4), dev(y=(y + 3) % 4)]

    def remote(src, dst, ss, rs, to):
        return pltpu.make_async_remote_copy(
            src_ref=src, dst_ref=dst, send_sem=ss, recv_sem=rs, device_id=to, device_id_type=MESH
        )

    loads = [
        pltpu.make_async_copy(q_hbm, q, in_sem.at[0]),
        pltpu.make_async_copy(k_hbm, k, in_sem.at[1]),
        pltpu.make_async_copy(v_hbm, v.at[:, pl.ds(0, HEAD)], in_sem.at[2]),
        pltpu.make_async_copy(w_hbm.at[:, pl.ds(pl.multiple_of(xh * WIDE, WIDE), WIDE)], wo, in_sem.at[3]),
    ]
    for load in loads:
        load.start()

    barrier = pltpu.get_barrier_semaphore()
    everyone = [d_kv, d_w, *d_z, d_c, d_a, *d_y]
    for other in everyone:
        pl.semaphore_signal(barrier, 1, device_id=other, device_id_type=MESH)
    pl.semaphore_wait(barrier, len(everyone))

    kv_out = []
    for part in range(2):
        rows = pl.ds(part * FAR, FAR)
        kv_out.append(remote(k_hbm.at[rows], kf.at[rows], kv_ss.at[part, 0], kv_rs.at[part, 0], d_kv))
        kv_out.append(
            remote(v_hbm.at[rows], vf.at[rows, pl.ds(0, HEAD)], kv_ss.at[part, 1], kv_rs.at[part, 1], d_kv)
        )

    @pl.when(xl == 0)
    def _():
        for copy in kv_out:
            copy.start()

    def piece(dz, first=0, count=PIECE):
        at = (((z + dz) % 4) * 2 + c) * PIECE + first
        return pl.ds(pl.multiple_of(at, 16), count)

    theirs = pl.ds(pl.multiple_of((1 - xh) * WIDE, WIDE), WIDE)
    w_x = remote(w_hbm.at[piece(0), theirs], wr.at[piece(0)], w_ss.at[0], w_rs.at[0], d_w)
    w_x.start()
    mine = [piece(0), piece(0), piece(0, 0, 32), piece(0, 32, 32)]
    w_z = [remote(wr.at[mine[i]], wr.at[mine[i]], w_ss.at[1 + i], w_rs.at[1 + i], d_z[i]) for i in range(4)]
    came = [piece(3), piece(1), piece(2, 0, 32), piece(2, 32, 32)]
    w_c = [
        remote(wr.at[rows], wr.at[rows], w_ss.at[5 + i], w_rs.at[5 + i], d_c)
        for i, rows in enumerate([piece(0), *came])
    ]

    ones = jnp.ones((TOK, HEAD), BF16)
    v[:, pl.ds(HEAD, HEAD)] = ones
    vf[:, pl.ds(HEAD, HEAD)] = ones
    for load in loads[:3]:
        load.wait()

    def finish(rows, h, o, m):
        l = o[:, HEAD:]
        att[rows, pl.ds(h * HEAD, HEAD)] = (o[:, :HEAD] / l).astype(BF16)
        top[h, rows, :] = (m + jnp.log2(l)) * LN2

    def own(qi):
        rows = pl.ds(qi * QC, QC)
        causal = lax.broadcasted_iota(jnp.int32, (QC, QC), 0) >= lax.broadcasted_iota(jnp.int32, (QC, QC), 1)
        for h in range(GROUP):
            qh = q[rows, pl.ds(h * HEAD, HEAD)]
            sd = jnp.where(causal, dot_nt(qh, k[rows, :]) * SCALE, -1e30)
            m = jnp.max(sd, axis=1, keepdims=True)
            if qi:
                before = pl.ds(0, qi * QC)
                sb = dot_nt(qh, k[before, :]) * SCALE
                m = jnp.maximum(m, jnp.max(sb, axis=1, keepdims=True))
            o = dot_nn(jnp.exp2(sd - m).astype(BF16), v[rows, :])
            if qi:
                o += dot_nn(jnp.exp2(sb - m).astype(BF16), v[before, :])
            m = jnp.broadcast_to(m, (QC, HEAD))
            acc[h, rows, :] = o
            top[h, rows, :] = m

    def far(part, qi):
        rows = pl.ds(pl.multiple_of(qi * QC, QC), QC)
        seen = pl.ds(part * FAR, FAR)
        for h in range(GROUP):
            sf = dot_nt(q[rows, pl.ds(h * HEAD, HEAD)], kf[seen, :]) * SCALE
            old = top[h, rows, :]
            m = jnp.maximum(old, jnp.broadcast_to(jnp.max(sf, axis=1, keepdims=True), (QC, HEAD)))
            keep = jnp.exp2(old - m)
            p = jnp.exp2(sf - jnp.concatenate([m] * (FAR // HEAD), axis=1))
            o = dot_nn(p.astype(BF16), vf[seen, :])
            o += acc[h, rows, :] * jnp.concatenate([keep, keep], axis=1)
            if part:
                finish(rows, h, o, m)
            else:
                acc[h, rows, :] = o
                top[h, rows, :] = m

    def a_copy(qi):
        rows = pl.ds(pl.multiple_of(qi * QC, QC), QC)
        return remote(att.at[rows], attp.at[rows], a_ss.at[qi], a_rs.at[qi], d_a)

    for qi in range(2):
        own(qi)
    w_x.wait_recv()
    for copy in w_z:
        copy.start()
    w_c[0].start()
    for qi in range(2, TOK // QC):
        own(qi)

    @pl.when(busy)
    def _():
        for copy in kv_out[:2]:
            copy.wait_recv()

        @pl.loop(0, TOK // QC)
        def _(qi):
            far(0, qi)

    for i in range(4):
        w_z[i].wait_recv()
        w_c[1 + i].start()

    @pl.when(busy)
    def _():
        for copy in kv_out[2:]:
            copy.wait_recv()

        @pl.loop(0, TOK // QC)
        def _(qi):
            far(1, qi)
            a_copy(qi).start()

    @pl.when(xl == 0)
    def _():
        @pl.loop(0, TOK // QC)
        def _(qi):
            rows = pl.ds(pl.multiple_of(qi * QC, QC), QC)
            for h in range(GROUP):
                finish(rows, h, acc[h, rows, :], top[h, rows, :])

        for copy in kv_out:
            copy.wait_send()

        @pl.loop(0, TOK // QC)
        def _(qi):
            a_copy(qi).start()

    loads[3].wait()
    for copy in w_c:
        copy.wait_recv()

    def part_of(i, block):
        rows = pl.ds(pl.multiple_of(i * STEP, STEP), STEP)
        cols = pl.ds(pl.multiple_of(block * BLK, BLK), BLK)
        return dot_nn(att[rows, :], wo[:, cols]) + dot_nn(attp[rows, :], wr[:, cols])

    def m1(i, way):
        rows = pl.ds(pl.multiple_of(i * STEP, STEP), STEP)
        return remote(m1s.at[way, rows], m1r.at[way, rows], s1_ss.at[way, i], s1_rs.at[way, i], d_y[way])

    def m2(i, way):
        rows = pl.ds(pl.multiple_of(i * STEP, STEP), STEP)
        return remote(m2s.at[way, rows], m2r.at[way, rows], s2_ss.at[way, i], s2_rs.at[way, i], d_y[way])

    def send_far(i):
        rows = pl.ds(pl.multiple_of(i * STEP, STEP), STEP)

        @pl.when(i % (QC // STEP) == 0)
        def _():
            a_copy(i // (QC // STEP)).wait_recv()

        f = part_of(i, (y + 2) % 4).astype(BF16)
        for way in range(2):
            m1s[way, rows, :] = f[:, way * HALF : (way + 1) * HALF]
            m1(i, way).start()

    def send_near(i):
        rows = pl.ds(pl.multiple_of(i * STEP, STEP), STEP)
        for way in range(2):
            f = part_of(i, (y + 1 + 2 * way) % 4)
            m1(i, way).wait_recv()
            for half in range(2):
                cols = pl.ds(half * HALF, HALF)
                mine = f[:, half * HALF : (half + 1) * HALF]
                if half == way:
                    mine += m1r[way, rows, :].astype(F32)
                m2s[way, rows, cols] = mine.astype(BF16)
            m2(i, way).start()

    def out_copy(i):
        rows = pl.ds(pl.multiple_of(i * STEP, STEP), STEP)
        return pltpu.make_async_copy(outv.at[rows], out_hbm.at[rows], out_sem.at[i])

    def collect(i):
        rows = pl.ds(pl.multiple_of(i * STEP, STEP), STEP)
        f = part_of(i, y)
        for way in range(2):
            m2(i, way).wait_recv()
            f += m2r[way, rows, :].astype(F32)
        outv[rows, :] = f.astype(BF16)
        out_copy(i).start()

    send_far(0)
    send_far(1)
    send_near(0)

    for h in range(GROUP):
        for qi in range(TOK // QC):
            rows = pl.ds(qi * QC, QC)
            lsev[pl.ds(h, 1), rows] = jnp.transpose(top[h, rows, :])[0:1, :]
    lse_copy = pltpu.make_async_copy(lsev, lse_hbm, out_sem.at[NSTEP])
    lse_copy.start()

    @pl.loop(2, NSTEP)
    def _(i):
        send_far(i)
        send_near(i - 1)
        collect(i - 2)

    send_near(NSTEP - 1)
    collect(NSTEP - 2)
    collect(NSTEP - 1)

    w_x.wait_send()
    for copy in [*w_z, *w_c]:
        copy.wait_send()

    @pl.loop(0, TOK // QC)
    def _(qi):
        a_copy(qi).wait_send()

    @pl.loop(0, NSTEP)
    def _(i):
        for way in range(2):
            m1(i, way).wait_send()
            m2(i, way).wait_send()
        out_copy(i).wait()

    lse_copy.wait()


def body(queries, keys, values, out_weight):
    dma = pltpu.SemaphoreType.DMA
    anywhere = pl.BlockSpec(memory_space=pl.ANY)
    return pl.pallas_call(
        kernel,
        out_shape=(
            jax.ShapeDtypeStruct((TOK, BLK), BF16),
            jax.ShapeDtypeStruct((GROUP, TOK), F32),
        ),
        in_specs=[anywhere] * 4,
        out_specs=(anywhere, anywhere),
        scratch_shapes=[
            pltpu.VMEM((TOK, BLK), BF16),
            pltpu.VMEM((TOK, HEAD), BF16),
            pltpu.VMEM((TOK, 2 * HEAD), BF16),
            pltpu.VMEM((TOK, HEAD), BF16),
            pltpu.VMEM((TOK, 2 * HEAD), BF16),
            pltpu.VMEM((BLK, WIDE), BF16),
            pltpu.VMEM((BLK, WIDE), BF16),
            pltpu.VMEM((TOK, BLK), BF16),
            pltpu.VMEM((TOK, BLK), BF16),
            pltpu.VMEM((GROUP, TOK, 2 * HEAD), F32),
            pltpu.VMEM((GROUP, TOK, HEAD), F32),
            pltpu.VMEM((2, TOK, HALF), BF16),
            pltpu.VMEM((2, TOK, HALF), BF16),
            pltpu.VMEM((2, TOK, BLK), BF16),
            pltpu.VMEM((2, TOK, BLK), BF16),
            pltpu.VMEM((TOK, BLK), BF16),
            pltpu.VMEM((GROUP, TOK), F32),
            dma((4,)),
            dma((NSTEP + 1,)),
            dma((2, 2)),
            dma((2, 2)),
            dma((10,)),
            dma((10,)),
            dma((TOK // QC,)),
            dma((TOK // QC,)),
            dma((2, NSTEP)),
            dma((2, NSTEP)),
            dma((2, NSTEP)),
            dma((2, NSTEP)),
        ],
        compiler_params=pltpu.CompilerParams(
            collective_id=0, has_side_effects=True, vmem_limit_bytes=60 * 2**20
        ),
        cost_estimate=pl.CostEstimate(flops=10**10, bytes_accessed=8 * 2**20, transcendentals=8 * 2**20),
    )(queries, keys, values, out_weight)


def solution(mesh):
    in_specs = (P("seq", "kvh"), P("seq", "kvh"), P("seq", "kvh"), P("kvh", None))
    out_specs = (P("seq", "kvh"), P("kvh", "seq"))
    return jax.shard_map(body, mesh=mesh, in_specs=in_specs, out_specs=out_specs, check_vma=False)
```

time: 181 us -> 79.5 us (0.44)
  waiting for transfers between devices: 121 us -> 0 us
  Pallas kernels: 0 us -> 75.1 us
  matrix products: 27.7 us -> 0 us
  between operations: 14.1 us -> 0.64 us
  other arithmetic: 11.9 us -> 0 us
  starting transfers between devices: 2.75 us -> 0 us
    reduce_scatter x1 -> x0, waiting for transfers between devices: 121 us -> none  [body(): lax.psum_scatter(term.astype(jnp.bfloat16), 'kvh', scatter_dimension=1, t...]
    pallas_call x0 -> x1, Pallas kernels: none -> 75.1 us  [body(): pl.pallas_call(kernel, out_shape=(jax.ShapeDtypeStruct((TOK, BLK), BF16),...]
    dot_general x9 -> x0, matrix products: 27.7 us -> none  [the longest x4 11.7 us: tile(): jnp.einsum('kgts,skd->kgtd', weights.astype(jnp.bfloat16), value_rows, pr...]
    reduce_sum x2 -> x0, other arithmetic: 6.99 us -> none  [tile(): total = jnp.sum(weights, axis=-1)]
    convert_element_type x1 -> x0, other arithmetic: 3.67 us -> none  [body(): attended = attended.astype(jnp.bfloat16)]
    unnamed x6 -> x2, local copies, waits for them, and re-layouts: 0.02 us -> 3.59 us
    ppermute x2 -> x0, starting transfers between devices: 2.72 us -> none  [passed_along(): lax.ppermute(value, axis, [(source, source + steps) for source in range(i...]
    cond x1 -> x0, local copies, waits for them, and re-layouts: 1.86 us -> none  [body(): results.append(lax.cond(busy, earlier, nothing))]
  transfers between devices with their start and end apart: 3 -> 0, of which waited for: 1 -> 0; matrix products, arithmetic and copies ran while one was open for 9% -> 0% of each run, Pallas kernels for 0% -> 0%
where the time goes in v1:
time: 79.5 us; the launch traced here: 79.3 us
  Pallas kernels  75.1 us (94%)
  local copies, waits for them, and re-layouts  3.59 us (5%)
    pallas_call x1, Pallas kernels, body(): pl.pallas_call(kernel, out_shape=(jax.ShapeDtypeStruct((TOK, BLK), BF16),...  75.1 us
    unnamed x2, local copies, waits for them, and re-layouts  3.59 us

profile of v1, /device:TPU:2, one launch (start us, length us, event | category | flops | bytes accessed | tf_op | source)
XLA Modules:
  0.0 79.3 jit_solution(3650962403129385960)
XLA Ops:
  0.6 75.1 %shard_map.59 = (bf16[1024,512]{1,0:T(8,128)(2,1)}, f32[4,1024]{1,0:T(4,128)}) custom-call(bf16[1024,512]{1,0:T(8,128)(2,1)} %q_hbm.1, bf16[1024,128]{1,0:T(8,128)(2,1)} %k_hbm.1, bf16[1024,128]{1,0:T(8,128)(2,1)} %v_hbm.1, bf16[512,4096]{1,0:T(8,128)(2,1)} %w_hbm.1), custom_call_target="tpu_custom_call" | custom-call | flops 10000000000 | bytes 8388608 | tf_op jit(solution)/shard_map/pallas_call | solution.py:301
  75.7 2.3 %copy.8 = bf16[1024,512]{1,0:T(8,128)(2,1)} copy(bf16[1024,512]{1,0:T(8,128)(2,1)} %get-tuple-element.4) | data formatting | bytes 2097152
  78.0 1.3 %copy.9 = f32[4,1024]{1,0:T(4,128)} copy(f32[4,1024]{1,0:T(4,128)} %get-tuple-element.5) | data formatting | bytes 32768

commit v2 on v1

v2 whole, which is shorter than its diff:
```python
import functools
import math

import jax
import jax.numpy as jnp
from jax import lax
from jax.experimental import pallas as pl
from jax.experimental.pallas import tpu as pltpu
from jax.sharding import PartitionSpec as P

MESH = pl.DeviceIdType.MESH
HEAD = 128
GROUP = 4
TOK = 1024
QC = 256
FAR = 256
PARTS = TOK // FAR
STEP = 128
NSTEP = TOK // STEP
BLK = 512
HALF = BLK // 2
WIDE = 4 * BLK
PIECE = 128
SCALE = math.log2(math.e) / math.sqrt(HEAD)
LN2 = math.log(2.0)
F32 = jnp.float32
BF16 = jnp.bfloat16


def dot_nt(a, b):
    return lax.dot_general(a, b, (((1,), (1,)), ((), ())), preferred_element_type=F32)


def dot_nn(a, b):
    return jnp.dot(a, b, preferred_element_type=F32)


def kernel(
    q_hbm, k_hbm, v_hbm, w_hbm, out, lse,
    q, k, v, kf, vf, w, att, acc, top, kept, xs, xr,
    in_sem, kv_ss, kv_rs, wy_ss, wy_rs, wz_ss, wz_rs, wc_ss, wc_rs, a_ss, a_rs, f_ss, f_rs, x_ss, x_rs,
):
    s = lax.axis_index("seq")
    g = lax.axis_index("kvh")
    xl, z, c = s // 16, (s // 2) % 8, s % 2
    xh, y = g // 4, g % 4
    busy = xl == 1

    def dev(xl=xl, z=z, c=c, xh=xh, y=y):
        return ((xl * 8 + z) * 2 + c, xh * 4 + y)

    zp = z % 2
    d_kv = dev(xl=1 - xl)
    d_z = dev(z=z + 1 - 2 * zp)
    d_c = dev(c=1 - c)
    d_x = dev(xh=1 - xh)
    ys = [(y + 1) % 4, (y + 3) % 4, (y + 2) % 4]
    d_y = [dev(y=other) for other in ys]

    def remote(src, dst, ss, rs, to):
        return pltpu.make_async_remote_copy(
            src_ref=src, dst_ref=dst, send_sem=ss, recv_sem=rs, device_id=to, device_id_type=MESH
        )

    def block_cols(b, owner):
        first = (xh if b == 0 else 1 - xh) * WIDE + owner * BLK
        return pl.ds(pl.multiple_of(first, BLK), BLK)

    loads = [
        pltpu.make_async_copy(q_hbm, q, in_sem.at[0]),
        pltpu.make_async_copy(k_hbm, k, in_sem.at[1]),
        pltpu.make_async_copy(v_hbm, v.at[:, pl.ds(0, HEAD)], in_sem.at[2]),
    ]
    w_loads = [
        pltpu.make_async_copy(w_hbm.at[:, block_cols(b, y)], w.at[3, b], in_sem.at[3 + b]) for b in range(2)
    ]
    for load in loads + w_loads:
        load.start()

    barrier = pltpu.get_barrier_semaphore()
    everyone = [d_kv, d_z, d_c, d_x, *d_y]
    for other in everyone:
        pl.semaphore_signal(barrier, 1, device_id=other, device_id_type=MESH)
    pl.semaphore_wait(barrier, len(everyone))

    kv = []
    for part in range(PARTS):
        rows = pl.ds(part * FAR, FAR)
        kv.append(
            (
                remote(k_hbm.at[rows], kf.at[rows], kv_ss.at[part, 0], kv_rs.at[part, 0], d_kv),
                remote(v_hbm.at[rows], vf.at[rows, pl.ds(0, HEAD)], kv_ss.at[part, 1], kv_rs.at[part, 1], d_kv),
            )
        )

    @pl.when(xl == 0)
    def _():
        for pair in kv:
            for copy in pair:
                copy.start()

    def quarter(zp, c):
        return pl.ds(pl.multiple_of((zp * 2 + c) * PIECE, PIECE), PIECE)

    mine, theirs = quarter(zp, c), quarter(1 - zp, c)
    wy = [
        [
            remote(w_hbm.at[mine, block_cols(b, ys[i])], w.at[i, b, mine], wy_ss.at[i, b], wy_rs.at[i, b], d_y[i])
            for b in range(2)
        ]
        for i in range(3)
    ]
    wz = [remote(w.at[i, :, mine], w.at[i, :, mine], wz_ss.at[i], wz_rs.at[i], d_z) for i in range(3)]
    wc = [
        [
            remote(w.at[i, :, rows], w.at[i, :, rows], wc_ss.at[j, i], wc_rs.at[j, i], d_c)
            for i in range(3)
        ]
        for j, rows in enumerate((mine, theirs))
    ]
    for pair in wy:
        for copy in pair:
            copy.start()

    def spread(i):
        for copy in wy[i]:
            copy.wait_recv()
        wz[i].start()
        wc[0][i].start()

    ones = jnp.ones((TOK, HEAD), BF16)
    v[:, pl.ds(HEAD, HEAD)] = ones
    vf[:, pl.ds(HEAD, HEAD)] = ones
    for load in loads:
        load.wait()

    def finish(rows, h, o, m):
        l = o[:, HEAD:]
        att[3, rows, pl.ds(h * HEAD, HEAD)] = (o[:, :HEAD] / l).astype(BF16)
        top[h, rows, :] = (m + jnp.log2(l)) * LN2

    def own(qi):
        rows = pl.ds(qi * QC, QC)
        causal = lax.broadcasted_iota(jnp.int32, (QC, QC), 0) >= lax.broadcasted_iota(jnp.int32, (QC, QC), 1)
        for h in range(GROUP):
            qh = q[rows, pl.ds(h * HEAD, HEAD)]
            sd = jnp.where(causal, dot_nt(qh, k[rows, :]) * SCALE, -1e30)
            m = jnp.max(sd, axis=1, keepdims=True)
            if qi:
                before = pl.ds(0, qi * QC)
                sb = dot_nt(qh, k[before, :]) * SCALE
                m = jnp.maximum(m, jnp.max(sb, axis=1, keepdims=True))
            o = dot_nn(jnp.exp2(sd - m).astype(BF16), v[rows, :])
            if qi:
                o += dot_nn(jnp.exp2(sb - m).astype(BF16), v[before, :])
            acc[h, rows, :] = o
            top[h, rows, :] = jnp.broadcast_to(m, (QC, HEAD))

    def far(part, qi):
        rows = pl.ds(pl.multiple_of(qi * QC, QC), QC)
        seen = pl.ds(part * FAR, FAR)
        for h in range(GROUP):
            sf = dot_nt(q[rows, pl.ds(h * HEAD, HEAD)], kf[seen, :]) * SCALE
            old = top[h, rows, :]
            m = jnp.maximum(old, jnp.broadcast_to(jnp.max(sf, axis=1, keepdims=True), (QC, HEAD)))
            keep = jnp.exp2(old - m)
            p = jnp.exp2(sf - jnp.concatenate([m] * (FAR // HEAD), axis=1))
            o = dot_nn(p.astype(BF16), vf[seen, :])
            o += acc[h, rows, :] * jnp.concatenate([keep, keep], axis=1)
            if part == PARTS - 1:
                finish(rows, h, o, m)
            else:
                acc[h, rows, :] = o
                top[h, rows, :] = m

    def step_rows(i):
        return pl.ds(pl.multiple_of(i * STEP, STEP), STEP)

    def direct(i, way):
        rows = step_rows(i)
        return remote(att.at[3, rows], att.at[way, rows], a_ss.at[way, i], a_rs.at[way, i], d_y[way])

    def forward(i, way):
        rows, cols = step_rows(i), pl.ds(way * HALF, HALF)
        return remote(
            att.at[way, rows, cols], att.at[2, rows, cols], f_ss.at[way, i], f_rs.at[way, i], d_y[way]
        )

    def send_direct(i):
        for way in range(2):
            direct(i, way).start()

    for qi in range(TOK // QC):
        own(qi)

    @pl.when(busy)
    def _():
        for part in range(PARTS - 1):
            for copy in kv[part]:
                copy.wait_recv()

            @pl.loop(0, TOK // QC)
            def _(qi):
                far(part, qi)

            if part == 1:
                spread(0)
                spread(1)

        for copy in kv[PARTS - 1]:
            copy.wait_recv()

        @pl.loop(0, TOK // QC)
        def _(qi):
            far(PARTS - 1, qi)

            @pl.when(qi == 0)
            def _():
                send_direct(0)
                send_direct(1)

    @pl.when(xl == 0)
    def _():
        @pl.loop(0, TOK // QC)
        def _(qi):
            rows = pl.ds(pl.multiple_of(qi * QC, QC), QC)
            for h in range(GROUP):
                finish(rows, h, acc[h, rows, :], top[h, rows, :])

            @pl.when(qi == 0)
            def _():
                send_direct(0)
                send_direct(1)

        spread(0)
        spread(1)

    spread(2)

    def pass_on(i):
        for way in range(2):
            direct(i, way).wait_recv()
            forward(i, way).start()

    def product(i, b):
        rows = step_rows(i)
        f = dot_nn(att[3, rows, :], w[3, b])
        for j in range(3):
            f += dot_nn(att[j, rows, :], w[j, b])
        return f

    def x_copy(i):
        rows = step_rows(i)
        return remote(xs.at[rows], xr.at[rows], x_ss.at[i], x_rs.at[i], d_x)

    def multiply(i):
        rows = step_rows(i)
        for way in range(2):
            forward(i, way).wait_recv()
        xs[rows, :] = product(i, 1).astype(BF16)
        x_copy(i).start()
        kept[rows, :] = product(i, 0)

    def collect(i):
        rows = step_rows(i)
        x_copy(i).wait_recv()
        out[rows, :] = (kept[rows, :] + xr[rows, :].astype(F32)).astype(BF16)

    pass_on(0)
    send_direct(2)
    pass_on(1)
    send_direct(3)

    for h in range(GROUP):
        for qi in range(TOK // QC):
            rows = pl.ds(qi * QC, QC)
            lse[pl.ds(h, 1), rows] = jnp.transpose(top[h, rows, :])[0:1, :]

    for i in range(3):
        wz[i].wait_recv()
        wc[1][i].start()
    for load in w_loads:
        load.wait()
    for j in range(2):
        for copy in wc[j]:
            copy.wait_recv()

    @pl.loop(2, NSTEP)
    def _(i):
        pass_on(i)

        @pl.when(i + 2 < NSTEP)
        def _():
            send_direct(i + 2)

        multiply(i - 2)

        @pl.when(i >= 4)
        def _():
            collect(i - 4)

    multiply(NSTEP - 2)
    multiply(NSTEP - 1)
    for i in range(NSTEP - 4, NSTEP):
        collect(i)

    @pl.when(xl == 0)
    def _():
        for pair in kv:
            for copy in pair:
                copy.wait_send()

    for copy in [*wy[0], *wy[1], *wy[2], *wz, *wc[0], *wc[1]]:
        copy.wait_send()

    @pl.loop(0, NSTEP)
    def _(i):
        for way in range(2):
            direct(i, way).wait_send()
            forward(i, way).wait_send()
        x_copy(i).wait_send()


def body(queries, keys, values, out_weight):
    dma = pltpu.SemaphoreType.DMA
    anywhere = pl.BlockSpec(memory_space=pl.ANY)
    return pl.pallas_call(
        kernel,
        out_shape=(
            jax.ShapeDtypeStruct((TOK, BLK), BF16),
            jax.ShapeDtypeStruct((GROUP, TOK), F32),
        ),
        in_specs=[anywhere] * 4,
        out_specs=(pl.BlockSpec(memory_space=pltpu.VMEM), pl.BlockSpec(memory_space=pltpu.VMEM)),
        scratch_shapes=[
            pltpu.VMEM((TOK, BLK), BF16),
            pltpu.VMEM((TOK, HEAD), BF16),
            pltpu.VMEM((TOK, 2 * HEAD), BF16),
            pltpu.VMEM((TOK, HEAD), BF16),
            pltpu.VMEM((TOK, 2 * HEAD), BF16),
            pltpu.VMEM((4, 2, BLK, BLK), BF16),
            pltpu.VMEM((4, TOK, BLK), BF16),
            pltpu.VMEM((GROUP, TOK, 2 * HEAD), F32),
            pltpu.VMEM((GROUP, TOK, HEAD), F32),
            pltpu.VMEM((TOK, BLK), F32),
            pltpu.VMEM((TOK, BLK), BF16),
            pltpu.VMEM((TOK, BLK), BF16),
            dma((5,)),
            dma((PARTS, 2)),
            dma((PARTS, 2)),
            dma((3, 2)),
            dma((3, 2)),
            dma((3,)),
            dma((3,)),
            dma((2, 3)),
            dma((2, 3)),
            dma((2, NSTEP)),
            dma((2, NSTEP)),
            dma((2, NSTEP)),
            dma((2, NSTEP)),
            dma((NSTEP,)),
            dma((NSTEP,)),
        ],
        compiler_params=pltpu.CompilerParams(
            collective_id=0, has_side_effects=True, vmem_limit_bytes=60 * 2**20
        ),
        cost_estimate=pl.CostEstimate(flops=10**10, bytes_accessed=8 * 2**20, transcendentals=8 * 2**20),
    )(queries, keys, values, out_weight)


def solution(mesh):
    in_specs = (P("seq", "kvh"), P("seq", "kvh"), P("seq", "kvh"), P("kvh", None))
    out_specs = (P("seq", "kvh"), P("kvh", "seq"))
    return jax.shard_map(body, mesh=mesh, in_specs=in_specs, out_specs=out_specs, check_vma=False)
```

time: 79.5 us -> 70.3 us (0.88); the launches traced: 79.3 us -> 68.9 us
  Pallas kernels: 75.1 us -> 64.7 us
    pallas_call x1, Pallas kernels: 75.1 us -> 64.7 us  [body(): pl.pallas_call(kernel, out_shape=(jax.ShapeDtypeStruct((TOK, BLK), BF16),...]
where the time goes in v2:
time: 70.3 us; the launch traced here: 68.9 us
  Pallas kernels  64.7 us (92%)
  local copies, waits for them, and re-layouts  3.59 us (5%)
    pallas_call x1, Pallas kernels, body(): pl.pallas_call(kernel, out_shape=(jax.ShapeDtypeStruct((TOK, BLK), BF16),...  64.7 us
    unnamed x2, local copies, waits for them, and re-layouts  3.59 us

profile of v2, /device:TPU:2, one launch (start us, length us, event | category | flops | bytes accessed | tf_op | source)
XLA Modules:
  0.0 68.9 jit_solution(8085918623770695823)
XLA Ops:
  0.6 64.7 %shard_map.59 = (bf16[1024,512]{1,0:T(8,128)(2,1)}, f32[4,1024]{1,0:T(4,128)}) custom-call(bf16[1024,512]{1,0:T(8,128)(2,1)} %q_hbm.1, bf16[1024,128]{1,0:T(8,128)(2,1)} %k_hbm.1, bf16[1024,128]{1,0:T(8,128)(2,1)} %v_hbm.1, bf16[512,4096]{1,0:T(8,128)(2,1)} %w_hbm.1), custom_call_target="tpu_custom_call" | custom-call | flops 10000000000 | bytes 8388608 | tf_op jit(solution)/shard_map/pallas_call | solution.py:327
  65.3 2.3 %copy.8 = bf16[1024,512]{1,0:T(8,128)(2,1)} copy(bf16[1024,512]{1,0:T(8,128)(2,1)} %get-tuple-element.4) | data formatting | bytes 2097152
  67.6 1.3 %copy.9 = f32[4,1024]{1,0:T(4,128)} copy(f32[4,1024]{1,0:T(4,128)} %get-tuple-element.5) | data formatting | bytes 32768

commit v3 on v2

--- a/solution.py
+++ b/solution.py
@@ -13,12 +13,15 @@
 GROUP = 4
 TOK = 1024
 QC = 256
-FAR = 256
+FAR = 512
 PARTS = TOK // FAR
 STEP = 128
 NSTEP = TOK // STEP
 BLK = 512
-HALF = BLK // 2
+HALF = STEP // 2
+AHEAD = 3
+LATE = NSTEP // 2
+LAG = LATE + 1
 WIDE = 4 * BLK
 PIECE = 128
 SCALE = math.log2(math.e) / math.sqrt(HEAD)
@@ -110,23 +113,37 @@
         ]
         for i in range(3)
     ]
-    wz = [remote(w.at[i, :, mine], w.at[i, :, mine], wz_ss.at[i], wz_rs.at[i], d_z) for i in range(3)]
+    wz = [
+        [remote(w.at[i, b, mine], w.at[i, b, mine], wz_ss.at[i, b], wz_rs.at[i, b], d_z) for b in range(2)]
+        for i in range(3)
+    ]
     wc = [
         [
-            remote(w.at[i, :, rows], w.at[i, :, rows], wc_ss.at[j, i], wc_rs.at[j, i], d_c)
+            [remote(w.at[i, b, rows], w.at[i, b, rows], wc_ss.at[j, i, b], wc_rs.at[j, i, b], d_c) for b in range(2)]
             for i in range(3)
         ]
         for j, rows in enumerate((mine, theirs))
     ]
-    for pair in wy:
-        for copy in pair:
-            copy.start()
-
-    def spread(i):
-        for copy in wy[i]:
-            copy.wait_recv()
-        wz[i].start()
-        wc[0][i].start()
+    for b in (1, 0):
+        for i in range(3):
+            wy[i][b].start()
+
+    def spread(b):
+        for i in range(3):
+            wy[i][b].wait_recv()
+            wz[i][b].start()
+            wc[0][i][b].start()
+
+    def gather(b):
+        for i in range(3):
+            wz[i][b].wait_recv()
+            wc[1][i][b].start()
+
+    def ready(b):
+        w_loads[b].wait()
+        for j in range(2):
+            for i in range(3):
+                wc[j][i][b].wait_recv()
 
     ones = jnp.ones((TOK, HEAD), BF16)
     v[:, pl.ds(HEAD, HEAD)] = ones
@@ -181,10 +198,8 @@
         return remote(att.at[3, rows], att.at[way, rows], a_ss.at[way, i], a_rs.at[way, i], d_y[way])
 
     def forward(i, way):
-        rows, cols = step_rows(i), pl.ds(way * HALF, HALF)
-        return remote(
-            att.at[way, rows, cols], att.at[2, rows, cols], f_ss.at[way, i], f_rs.at[way, i], d_y[way]
-        )
+        rows = pl.ds(pl.multiple_of(i * STEP + way * HALF, HALF), HALF)
+        return remote(att.at[way, rows], att.at[2, rows], f_ss.at[way, i], f_rs.at[way, i], d_y[way])
 
     def send_direct(i):
         for way in range(2):
@@ -195,6 +210,7 @@
 
     @pl.when(busy)
     def _():
+        spread(1)
         for part in range(PARTS - 1):
             for copy in kv[part]:
                 copy.wait_recv()
@@ -203,10 +219,6 @@
             def _(qi):
                 far(part, qi)
 
-            if part == 1:
-                spread(0)
-                spread(1)
-
         for copy in kv[PARTS - 1]:
             copy.wait_recv()
 
@@ -214,10 +226,11 @@
         def _(qi):
             far(PARTS - 1, qi)
 
-            @pl.when(qi == 0)
-            def _():
-                send_direct(0)
-                send_direct(1)
+            for i in range(AHEAD):
+
+                @pl.when(qi == i * STEP // QC)
+                def _():
+                    send_direct(i)
 
     @pl.when(xl == 0)
     def _():
@@ -227,15 +240,15 @@
             for h in range(GROUP):
                 finish(rows, h, acc[h, rows, :], top[h, rows, :])
 
-            @pl.when(qi == 0)
-            def _():
-                send_direct(0)
-                send_direct(1)
-
-        spread(0)
+            for i in range(AHEAD):
+
+                @pl.when(qi == i * STEP // QC)
+                def _():
+                    send_direct(i)
+
         spread(1)
 
-    spread(2)
+    spread(0)
 
     def pass_on(i):
         for way in range(2):
@@ -253,55 +266,71 @@
         rows = step_rows(i)
         return remote(xs.at[rows], xr.at[rows], x_ss.at[i], x_rs.at[i], d_x)
 
-    def multiply(i):
-        rows = step_rows(i)
+    def multiply_theirs(i):
         for way in range(2):
             forward(i, way).wait_recv()
-        xs[rows, :] = product(i, 1).astype(BF16)
+        xs[step_rows(i), :] = product(i, 1).astype(BF16)
         x_copy(i).start()
-        kept[rows, :] = product(i, 0)
+
+    def multiply_mine(i):
+        kept[step_rows(i), :] = product(i, 0)
 
     def collect(i):
         rows = step_rows(i)
         x_copy(i).wait_recv()
         out[rows, :] = (kept[rows, :] + xr[rows, :].astype(F32)).astype(BF16)
 
-    pass_on(0)
-    send_direct(2)
-    pass_on(1)
-    send_direct(3)
+    for i in range(2):
+        pass_on(i)
+        send_direct(i + AHEAD)
 
     for h in range(GROUP):
         for qi in range(TOK // QC):
             rows = pl.ds(qi * QC, QC)
             lse[pl.ds(h, 1), rows] = jnp.transpose(top[h, rows, :])[0:1, :]
 
-    for i in range(3):
-        wz[i].wait_recv()
-        wc[1][i].start()
-    for load in w_loads:
-        load.wait()
-    for j in range(2):
-        for copy in wc[j]:
-            copy.wait_recv()
+    gather(1)
+    ready(1)
 
     @pl.loop(2, NSTEP)
     def _(i):
         pass_on(i)
 
-        @pl.when(i + 2 < NSTEP)
+        @pl.when(i + AHEAD < NSTEP)
         def _():
-            send_direct(i + 2)
-
-        multiply(i - 2)
-
-        @pl.when(i >= 4)
+            send_direct(i + AHEAD)
+
+        multiply_theirs(i - 2)
+
+        @pl.when(i == LATE - 1)
         def _():
-            collect(i - 4)
-
-    multiply(NSTEP - 2)
-    multiply(NSTEP - 1)
-    for i in range(NSTEP - 4, NSTEP):
+            gather(0)
+
+        @pl.when(i == LATE)
+        def _():
+            ready(0)
+
+        @pl.when(i >= LATE)
+        def _():
+            for j in range(2):
+                at = 2 * (i - LATE) + j
+
+                @pl.when(at <= i - 2)
+                def _():
+                    multiply_mine(at)
+
+        @pl.when(i >= LAG)
+        def _():
+            collect(i - LAG)
+
+    multiply_theirs(NSTEP - 2)
+    multiply_mine(NSTEP - 3)
+    for i in range(NSTEP - LAG, NSTEP - 3):
+        collect(i)
+    multiply_theirs(NSTEP - 1)
+    multiply_mine(NSTEP - 2)
+    multiply_mine(NSTEP - 1)
+    for i in range(NSTEP - 3, NSTEP):
         collect(i)
 
     @pl.when(xl == 0)
@@ -310,8 +339,10 @@
             for copy in pair:
                 copy.wait_send()
 
-    for copy in [*wy[0], *wy[1], *wy[2], *wz, *wc[0], *wc[1]]:
-        copy.wait_send()
+    for i in range(3):
+        for b in range(2):
+            for copy in (wy[i][b], wz[i][b], wc[0][i][b], wc[1][i][b]):
+                copy.wait_send()
 
     @pl.loop(0, NSTEP)
     def _(i):
@@ -327,8 +358,8 @@
     return pl.pallas_call(
         kernel,
         out_shape=(
-            jax.ShapeDtypeStruct((TOK, BLK), BF16),
-            jax.ShapeDtypeStruct((GROUP, TOK), F32),
+            pltpu.VMEM((TOK, BLK), BF16),
+            pltpu.VMEM((GROUP, TOK), F32),
         ),
         in_specs=[anywhere] * 4,
         out_specs=(pl.BlockSpec(memory_space=pltpu.VMEM), pl.BlockSpec(memory_space=pltpu.VMEM)),
@@ -350,10 +381,10 @@
             dma((PARTS, 2)),
             dma((3, 2)),
             dma((3, 2)),
-            dma((3,)),
-            dma((3,)),
-            dma((2, 3)),
-            dma((2, 3)),
+            dma((3, 2)),
+            dma((3, 2)),
+            dma((2, 3, 2)),
+            dma((2, 3, 2)),
             dma((2, NSTEP)),
             dma((2, NSTEP)),
             dma((2, NSTEP)),

time: 70.3 us -> 64.9 us (0.923)
  Pallas kernels: 64.7 us -> 62 us
  local copies, waits for them, and re-layouts: 3.59 us -> 1.58 us
    pallas_call x1, Pallas kernels: 64.7 us -> 62 us  [body(): pl.pallas_call(kernel, out_shape=(pltpu.VMEM((TOK, BLK), BF16), pltpu.VME...]
    unnamed x2, local copies, waits for them, and re-layouts: 3.59 us -> 1.58 us
where the time goes in v3:
time: 64.9 us; the launch traced here: 64.2 us
  Pallas kernels  62 us (96%)
  local copies, waits for them, and re-layouts  1.58 us (2%)
    pallas_call x1, Pallas kernels, body(): pl.pallas_call(kernel, out_shape=(pltpu.VMEM((TOK, BLK), BF16), pltpu.VME...  62 us
    unnamed x2, local copies, waits for them, and re-layouts  1.58 us

profile of v3, /device:TPU:2, one launch (start us, length us, event | category | flops | bytes accessed | tf_op | source)
XLA Modules:
  0.0 64.2 jit_solution(5817118796226059703)
XLA Ops:
  0.6 62.0 %shard_map.59 = (bf16[1024,512]{1,0:T(8,128)(2,1)S(1)}, f32[4,1024]{1,0:T(4,128)S(1)}) custom-call(bf16[1024,512]{1,0:T(8,128)(2,1)} %q_hbm.1, bf16[1024,128]{1,0:T(8,128)(2,1)} %k_hbm.1, bf16[1024,128]{1,0:T(8,128)(2,1)} %v_hbm.1, bf16[512,4096]{1,0:T(8,128)(2,1)} %w_hbm.1), custom_call_target="tpu_custom_call" | custom-call | flops 10000000000 | bytes 8388608 | tf_op jit(solution)/shard_map/pallas_call | solution.py:358
  62.6 1.0 %copy.8 = bf16[1024,512]{1,0:T(8,128)(2,1)} copy(bf16[1024,512]{1,0:T(8,128)(2,1)S(1)} %get-tuple-element.2) | data formatting | bytes 2097152
  63.6 0.6 copy.9

commit v4 on v3

--- a/solution.py
+++ b/solution.py
@@ -16,11 +16,12 @@
 FAR = 512
 PARTS = TOK // FAR
 STEP = 128
-NSTEP = TOK // STEP
 BLK = 512
-HALF = STEP // 2
+FULL = 7
+TAIL = 64
+NCHUNK = FULL + (TOK - FULL * STEP) // TAIL
 AHEAD = 3
-LATE = NSTEP // 2
+LATE = 4
 LAG = LATE + 1
 WIDE = 4 * BLK
 PIECE = 128
@@ -41,7 +42,7 @@
 def kernel(
     q_hbm, k_hbm, v_hbm, w_hbm, out, lse,
     q, k, v, kf, vf, w, att, acc, top, kept, xs, xr,
-    in_sem, kv_ss, kv_rs, wy_ss, wy_rs, wz_ss, wz_rs, wc_ss, wc_rs, a_ss, a_rs, f_ss, f_rs, x_ss, x_rs,
+    in_sem, kv_ss, kv_rs, wy_ss, wy_rs, wx_ss, wx_rs, wz_ss, wz_rs, wc_ss, wc_rs, a_ss, a_rs, f_ss, f_rs, x_ss, x_rs,
 ):
     s = lax.axis_index("seq")
     g = lax.axis_index("kvh")
@@ -124,13 +125,18 @@
         ]
         for j, rows in enumerate((mine, theirs))
     ]
-    for b in (1, 0):
+    wx = [remote(w.at[i, 0, mine], w.at[i, 0, mine], wx_ss.at[i], wx_rs.at[i], d_kv) for i in range(3)]
+    for i in range(3):
+        wy[i][1].start()
+
+    @pl.when(busy)
+    def _():
         for i in range(3):
-            wy[i][b].start()
-
-    def spread(b):
+            wy[i][0].start()
+
+    def spread(b, source=None):
         for i in range(3):
-            wy[i][b].wait_recv()
+            (wy[i][b] if source is None else source[i]).wait_recv()
             wz[i][b].start()
             wc[0][i][b].start()
 
@@ -190,15 +196,21 @@
                 acc[h, rows, :] = o
                 top[h, rows, :] = m
 
-    def step_rows(i):
-        return pl.ds(pl.multiple_of(i * STEP, STEP), STEP)
+    def step_rows(i, part=None):
+        if isinstance(i, int) and i >= FULL:
+            first, size = FULL * STEP + (i - FULL) * TAIL, TAIL
+        else:
+            first, size = i * STEP, STEP
+        if part is not None:
+            first, size = first + part * (size // 2), size // 2
+        return pl.ds(first if isinstance(first, int) else pl.multiple_of(first, size), size)
 
     def direct(i, way):
         rows = step_rows(i)
         return remote(att.at[3, rows], att.at[way, rows], a_ss.at[way, i], a_rs.at[way, i], d_y[way])
 
     def forward(i, way):
-        rows = pl.ds(pl.multiple_of(i * STEP + way * HALF, HALF), HALF)
+        rows = step_rows(i, way)
         return remote(att.at[way, rows], att.at[2, rows], f_ss.at[way, i], f_rs.at[way, i], d_y[way])
 
     def send_direct(i):
@@ -248,7 +260,11 @@
 
         spread(1)
 
-    spread(0)
+    @pl.when(busy)
+    def _():
+        spread(0)
+        for copy in wx:
+            copy.start()
 
     def pass_on(i):
         for way in range(2):
@@ -292,25 +308,35 @@
     gather(1)
     ready(1)
 
-    @pl.loop(2, NSTEP)
+    @pl.loop(2, FULL)
     def _(i):
         pass_on(i)
 
-        @pl.when(i + AHEAD < NSTEP)
+        @pl.when(i + AHEAD < FULL)
         def _():
             send_direct(i + AHEAD)
 
+        for chunk in range(FULL, NCHUNK):
+
+            @pl.when(i + AHEAD == chunk)
+            def _():
+                send_direct(chunk)
+
         multiply_theirs(i - 2)
 
-        @pl.when(i == LATE - 1)
+        @pl.when((i == LATE) & (xl == 0))
+        def _():
+            spread(0, wx)
+
+        @pl.when(i == LATE + 2 - 3 * xl)
         def _():
             gather(0)
 
-        @pl.when(i == LATE)
+        @pl.when((i == LATE) & busy)
         def _():
             ready(0)
 
-        @pl.when(i >= LATE)
+        @pl.when((i >= LATE) & busy)
         def _():
             for j in range(2):
                 at = 2 * (i - LATE) + j
@@ -319,18 +345,39 @@
                 def _():
                     multiply_mine(at)
 
-        @pl.when(i >= LAG)
+        @pl.when((i >= LAG) & busy)
         def _():
             collect(i - LAG)
 
-    multiply_theirs(NSTEP - 2)
-    multiply_mine(NSTEP - 3)
-    for i in range(NSTEP - LAG, NSTEP - 3):
-        collect(i)
-    multiply_theirs(NSTEP - 1)
-    multiply_mine(NSTEP - 2)
-    multiply_mine(NSTEP - 1)
-    for i in range(NSTEP - 3, NSTEP):
+    pass_on(7)
+    multiply_theirs(5)
+
+    @pl.when(xl == 0)
+    def _():
+        ready(0)
+
+        @pl.loop(0, LATE + 1)
+        def _(i):
+            multiply_mine(i)
+
+    multiply_mine(5)
+    collect(2)
+    pass_on(8)
+    multiply_theirs(6)
+
+    @pl.when(xl == 0)
+    def _():
+        collect(0)
+        collect(1)
+
+    multiply_theirs(7)
+    multiply_mine(6)
+    collect(3)
+    collect(4)
+    multiply_theirs(8)
+    multiply_mine(7)
+    multiply_mine(8)
+    for i in range(5, NCHUNK):
         collect(i)
 
     @pl.when(xl == 0)
@@ -341,15 +388,24 @@
 
     for i in range(3):
         for b in range(2):
-            for copy in (wy[i][b], wz[i][b], wc[0][i][b], wc[1][i][b]):
+            for copy in (wz[i][b], wc[0][i][b], wc[1][i][b]):
                 copy.wait_send()
-
-    @pl.loop(0, NSTEP)
-    def _(i):
+        wy[i][1].wait_send()
+
+        @pl.when(busy)
+        def _():
+            wy[i][0].wait_send()
+            wx[i].wait_send()
+
+    def sent(i):
         for way in range(2):
             direct(i, way).wait_send()
             forward(i, way).wait_send()
         x_copy(i).wait_send()
+
+    pl.loop(0, FULL)(sent)
+    for i in range(FULL, NCHUNK):
+        sent(i)
 
 
 def body(queries, keys, values, out_weight):
@@ -381,16 +437,18 @@
             dma((PARTS, 2)),
             dma((3, 2)),
             dma((3, 2)),
+            dma((3,)),
+            dma((3,)),
             dma((3, 2)),
             dma((3, 2)),
             dma((2, 3, 2)),
             dma((2, 3, 2)),
-            dma((2, NSTEP)),
-            dma((2, NSTEP)),
-            dma((2, NSTEP)),
-            dma((2, NSTEP)),
-            dma((NSTEP,)),
-            dma((NSTEP,)),
+            dma((2, NCHUNK)),
+            dma((2, NCHUNK)),
+            dma((2, NCHUNK)),
+            dma((2, NCHUNK)),
+            dma((NCHUNK,)),
+            dma((NCHUNK,)),
         ],
         compiler_params=pltpu.CompilerParams(
             collective_id=0, has_side_effects=True, vmem_limit_bytes=60 * 2**20

time: 64.9 us -> 64.1 us (0.988)
  no operation moved by 1% of the time
where the time goes in v4:
time: 64.1 us; the launch traced here: 64 us
  Pallas kernels  61.8 us (96%)
  local copies, waits for them, and re-layouts  1.58 us (2%)
    pallas_call x1, Pallas kernels, body(): pl.pallas_call(kernel, out_shape=(pltpu.VMEM((TOK, BLK), BF16), pltpu.VME...  61.8 us
    unnamed x2, local copies, waits for them, and re-layouts  1.58 us

profile of v4, /device:TPU:2, one launch (start us, length us, event | category | flops | bytes accessed | tf_op | source)
XLA Modules:
  0.0 64.0 jit_solution(263033491107300472)
XLA Ops:
  0.6 61.8 %shard_map.59 = (bf16[1024,512]{1,0:T(8,128)(2,1)S(1)}, f32[4,1024]{1,0:T(4,128)S(1)}) custom-call(bf16[1024,512]{1,0:T(8,128)(2,1)} %q_hbm.1, bf16[1024,128]{1,0:T(8,128)(2,1)} %k_hbm.1, bf16[1024,128]{1,0:T(8,128)(2,1)} %v_hbm.1, bf16[512,4096]{1,0:T(8,128)(2,1)} %w_hbm.1), custom_call_target="tpu_custom_call" | custom-call | flops 10000000000 | bytes 8388608 | tf_op jit(solution)/shard_map/pallas_call | solution.py:414
  62.4 1.0 %copy.8 = bf16[1024,512]{1,0:T(8,128)(2,1)} copy(bf16[1024,512]{1,0:T(8,128)(2,1)S(1)} %get-tuple-element.2) | data formatting | bytes 2097152
  63.4 0.6 copy.9

commit v5 on v4

--- a/solution.py
+++ b/solution.py
@@ -12,7 +12,7 @@
 HEAD = 128
 GROUP = 4
 TOK = 1024
-QC = 256
+QC = 128
 FAR = 512
 PARTS = TOK // FAR
 STEP = 128
@@ -222,7 +222,6 @@
 
     @pl.when(busy)
     def _():
-        spread(1)
         for part in range(PARTS - 1):
             for copy in kv[part]:
                 copy.wait_recv()
@@ -231,6 +230,7 @@
             def _(qi):
                 far(part, qi)
 
+        spread(1)
         for copy in kv[PARTS - 1]:
             copy.wait_recv()
 
@@ -318,7 +318,7 @@
 
         for chunk in range(FULL, NCHUNK):
 
-            @pl.when(i + AHEAD == chunk)
+            @pl.when(i + AHEAD - 1 == chunk)
             def _():
                 send_direct(chunk)
 
@@ -351,6 +351,8 @@
 
     pass_on(7)
     multiply_theirs(5)
+    multiply_theirs(6)
+    pass_on(8)
 
     @pl.when(xl == 0)
     def _():
@@ -360,24 +362,17 @@
         def _(i):
             multiply_mine(i)
 
-    multiply_mine(5)
-    collect(2)
-    pass_on(8)
-    multiply_theirs(6)
-
-    @pl.when(xl == 0)
-    def _():
         collect(0)
         collect(1)
 
+    multiply_mine(5)
     multiply_theirs(7)
-    multiply_mine(6)
+    collect(2)
+    multiply_theirs(8)
     collect(3)
-    collect(4)
-    multiply_theirs(8)
-    multiply_mine(7)
-    multiply_mine(8)
-    for i in range(5, NCHUNK):
+    for i in range(6, NCHUNK):
+        multiply_mine(i)
+    for i in range(4, NCHUNK):
         collect(i)
 
     @pl.when(xl == 0)

time: 64.1 us -> 63.2 us (0.986)
  Pallas kernels: 61.8 us -> 60.5 us
    pallas_call x1, Pallas kernels: 61.8 us -> 60.5 us  [body(): pl.pallas_call(kernel, out_shape=(pltpu.VMEM((TOK, BLK), BF16), pltpu.VME...]
where the time goes in v5:
time: 63.2 us; the launch traced here: 62.8 us
  Pallas kernels  60.5 us (96%)
  local copies, waits for them, and re-layouts  1.58 us (2%)
  between operations  0.64 us (1%)
    pallas_call x1, Pallas kernels, body(): pl.pallas_call(kernel, out_shape=(pltpu.VMEM((TOK, BLK), BF16), pltpu.VME...  60.5 us
    unnamed x2, local copies, waits for them, and re-layouts  1.58 us

profile of v5, /device:TPU:2, one launch (start us, length us, event | category | flops | bytes accessed | tf_op | source)
XLA Modules:
  0.0 62.8 jit_solution(255855796555989273)
XLA Ops:
  0.6 60.5 %shard_map.59 = (bf16[1024,512]{1,0:T(8,128)(2,1)S(1)}, f32[4,1024]{1,0:T(4,128)S(1)}) custom-call(bf16[1024,512]{1,0:T(8,128)(2,1)} %q_hbm.1, bf16[1024,128]{1,0:T(8,128)(2,1)} %k_hbm.1, bf16[1024,128]{1,0:T(8,128)(2,1)} %v_hbm.1, bf16[512,4096]{1,0:T(8,128)(2,1)} %w_hbm.1), custom_call_target="tpu_custom_call" | custom-call | flops 10000000000 | bytes 8388608 | tf_op jit(solution)/shard_map/pallas_call | solution.py:409
  61.2 1.0 %copy.8 = bf16[1024,512]{1,0:T(8,128)(2,1)} copy(bf16[1024,512]{1,0:T(8,128)(2,1)S(1)} %get-tuple-element.2) | data formatting | bytes 2097152
  62.2 0.6 copy.9
